TPU v7x, 32 devices: a whole 2x2x4 slice. The times are simulated.
32 devices in a mesh: groups: 2 (over y), ep: 8 (over z, x), sub: 2 (over core).
Axes of the slice: x: 2, y: 2, z: 4, core: 2. Of those that a mesh axis runs over, the one named last changes fastest.
Arguments:
- queries: bfloat16 [128, 4, 128, 576], P(('groups', 'ep', 'sub')), parts along dimension 0, may hold values from -8.25 to 8.25, as said below
- draft_keys: bfloat16 [128, 4, 576], P(('groups', 'ep', 'sub')), parts along dimension 0, may hold values from -6 to 6, as said below
- page_pool: bfloat16 [8192, 16, 576], P(('groups', 'ep', 'sub')), parts along dimension 0, may hold values from -6 to 6
- send_slot: int32 [32, 16], P(('groups', 'ep', 'sub')), parts along dimension 0, may hold values from -1 to 255, as said below
- page_table: int32 [128, 64], P(('groups', 'ep', 'sub')), parts along dimension 0, may hold values from 0 to 271, as said below
- cache_length: int32 [128], P(('groups', 'ep', 'sub')), parts along dimension 0, may hold values from 1 to 1024, as said below
- value_up_matrix: bfloat16 [128, 512, 128], P(('ep', 'sub')), may hold values from -0.25 to 0.25
Outputs:
- head_values: bfloat16 [128, 4, 16384], P(('groups', 'ep', 'sub')), parts along dimension 0
There are 2 independent parts, one for each index of `groups`. A program takes and returns all parts, laid end to end along the dimension named above; an argument that names none is the same for every part. Nothing has to cross between parts.
Inputs may be any that keep to these rules, and one draw needn't show every extreme that they name: `queries`: queries of order one. `draft_keys`: keys of order one. `send_slot`: each device sends exactly 15 pages, at most one to any other device and none to itself, each page at most once, and each device receives exactly 15 pages; a page that a device sends is not named in its own page_table rows. `page_table`: an entry e < 256 names page e of the device's own pages, an entry 256 + p the page received from device p; the 4 rows of one device name every page that the device holds after the migration (its unsent pages and the 15 received ones) exactly once. `cache_length`: some request holds 1024 accepted tokens and some holds 1.
All inputs are finite; a program needn't handle non-finite values.
Results may differ from a plain program's by a relative error of at most 0.0057.
Values may be sent and summed in bfloat16 or wider, within the bound.
A program may use at most 128 MiB of HBM per device.

v0:
```python
import jax
import jax.numpy as jnp
from jax import lax
from jax.sharding import PartitionSpec as P

LATENT_WIDTH = 512


score_scale = 192 ** (-0.5)


def attend(request_query, draft_key, page_rows, length, page_store):
    draft_token_count, head_number, key_width = request_query.shape
    cache_keys = page_store[page_rows].reshape(-1, key_width)
    context = cache_keys.shape[0]
    key_rows_all = jnp.concatenate([cache_keys, draft_key], axis=0)
    score_rows = request_query.reshape(draft_token_count * head_number, key_width)
    scores = jnp.dot(score_rows, key_rows_all.T, preferred_element_type=jnp.float32) * score_scale
    column_index = jnp.arange(context + draft_token_count, dtype=jnp.int32)[None, :]
    row_draft = (jnp.arange(draft_token_count * head_number, dtype=jnp.int32) // head_number)[
        :, None
    ]
    live_mask = jnp.where(
        column_index < context, column_index < length, column_index - context <= row_draft
    )
    scores = jnp.where(live_mask, scores, -jnp.inf)
    row_top = jnp.max(scores, axis=1, keepdims=True)
    exponent = jnp.exp(scores - row_top)
    row_total = jnp.sum(exponent, axis=1, keepdims=True)
    softmax_weight = (exponent / row_total).astype(jnp.bfloat16)
    latent_state = jnp.dot(
        softmax_weight, key_rows_all[:, :LATENT_WIDTH], preferred_element_type=jnp.float32
    ).astype(jnp.bfloat16)
    return latent_state.reshape(draft_token_count, head_number, LATENT_WIDTH)


def per_device(
    queries, draft_keys, page_pool, send_slot, page_table, cache_length, value_up_matrix
):
    picked = send_slot[0]
    outgoing = jnp.where(
        (picked >= 0)[:, None, None],
        page_pool[jnp.maximum(picked, 0)],
        jnp.zeros((), page_pool.dtype),
    )
    received = lax.all_to_all(outgoing, ("ep", "sub"), split_axis=0, concat_axis=0, tiled=True)
    page_store = jnp.concatenate([page_pool, received], axis=0)

    def one_request(inputs):
        return attend(inputs[0], inputs[1], inputs[2], inputs[3], page_store)

    latent_state = lax.map(one_request, (queries, draft_keys, page_table, cache_length))
    mixed_heads = jnp.einsum(
        "rjhc,hcv->rjhv",
        latent_state,
        lax.all_gather(value_up_matrix, ("ep", "sub"), axis=0, tiled=True),
        preferred_element_type=jnp.float32,
    ).astype(jnp.bfloat16)
    return mixed_heads.reshape(mixed_heads.shape[0], mixed_heads.shape[1], -1)


def solution(mesh):
    placed = (
        P(("groups", "ep", "sub"), None, None, None),
        P(("groups", "ep", "sub"), None, None),
        P(("groups", "ep", "sub"), None, None),
        P(("groups", "ep", "sub"), None),
        P(("groups", "ep", "sub"), None),
        P(("groups", "ep", "sub")),
        P(("ep", "sub"), None, None),
    )
    return jax.shard_map(
        per_device,
        mesh=mesh,
        in_specs=placed,
        out_specs=P(("groups", "ep", "sub"), None, None),
        check_vma=False,
    )
```

profile of v0, /device:TPU:0, one launch (start us, length us, event | category | flops | bytes accessed | tf_op | source)
XLA Modules:
  0.0 161.2 jit_solution(5687113635150369354)
XLA Ops:
  6.5 0.7 all-gather.2.cloned.1.call-update
  7.3 9.0 %copy.16 = bf16[256,16,576]{2,1,0:T(8,128)(2,1)} copy(bf16[256,16,576]{0,2,1:T(8,128)(2,1)} %param.11) | data formatting | bytes 9437184 | tf_op args[2]
  16.2 3.1 %gather_fusion.1 = bf16[16,16,576]{2,1,0:T(8,128)(2,1)S(1)} fusion(bf16[256,16,576]{2,1,0:T(8,128)(2,1)} %copy.16, s32[1024]{0:T(1024)S(1)} %pad_clamp_fusion.1), kind=kCustom, calls=%fused_computation.1 | custom fusion | bytes 589888 | tf_op jit(solution)/shard_map/gather | solution.py:43
  19.3 0.8 broadcast_select_fusion
  20.2 7.7 %all-to-all-start = ((bf16[16,16,576]{2,1,0:T(8,128)(2,1)}), bf16[16,16,576]{2,1,0:T(8,128)(2,1)S(1)}, u32[]{:S(2)}, u32[]{:S(2)}) async-start(bf16[16,16,576]{2,1,0:T(8,128)(2,1)} %broadcast_select_fusion), calls=%async_computation | async-start | bytes 655360 | tf_op jit(solution)/shard_map/all_to_all | solution.py:46
  27.9 16.7 %all-to-all-done = bf16[16,16,576]{2,1,0:T(8,128)(2,1)S(1)} async-done(((bf16[16,16,576]{2,1,0:T(8,128)(2,1)}), bf16[16,16,576]{2,1,0:T(8,128)(2,1)S(1)}, u32[]{:S(2)}, u32[]{:S(2)}) %all-to-all-start) | async-done | bytes 294944 | tf_op jit(solution)/shard_map/all_to_all | solution.py:46
  44.6 5.7 %pad_maximum_fusion = bf16[272,16,576]{2,1,0:T(8,128)(2,1)} fusion(bf16[16,16,576]{2,1,0:T(8,128)(2,1)S(1)} %all-to-all-done, bf16[256,16,576]{2,1,0:T(8,128)(2,1)} %copy.16), kind=kLoop, calls=%fused_computation.38 | loop fusion | flops 2506752 | bytes 10027008 | tf_op jit(solution)/shard_map/concatenate | solution.py:47
  50.3 42.5 %while.12 = (s32[]{:T(128)}, bf16[4,4,128,512]{3,1,0,2:T(4,128)(2,1)S(1)}, s32[4]{0:T(128)S(1)}, bf16[4,4,128,576]{2,3,1,0:T(8,128)(2,1)}, s32[4,64]{1,0:T(4,128...) while((s32[]{:T(128)}, bf16[4,4,128,512]{3,1,0,2:T(4,128)(2,1)S(1)}, ...), condition=%wide.region_3.4_spmd, body=%wide.region_0.3_spmd.sunk | while | flops 1155313920 | bytes 15606949 | solution.py:52
  51.0 3.4 %gather_fusion = bf16[64,16,576]{2,1,0:T(8,128)(2,1)S(1)} fusion(bf16[272,16,576]{2,1,0:T(8,128)(2,1)} %get-tuple-element.201, s32[1024]{0:T(1024)S(1)} %pad_clamp_fusion.3), kind=kCustom, calls=%fused_computation.clone.1 | custom fusion | bytes 2359552 | tf_op jit(solution)/shard_map/while/body/eval_jaxpr/gather | solution.py:14
  54.4 0.7 dynamic-slice_bitcast_fusion.2
  56.4 1.1 constant_dynamic-slice_fusion.3
  58.0 1.2 fusion.33
  59.5 0.9 convolution_convert_fusion.2
  61.6 3.4 %gather_fusion = bf16[64,16,576]{2,1,0:T(8,128)(2,1)S(1)} fusion(bf16[272,16,576]{2,1,0:T(8,128)(2,1)} %get-tuple-element.201, s32[1024]{0:T(1024)S(1)} %pad_clamp_fusion.3), kind=kCustom, calls=%fused_computation.clone.1 | custom fusion | bytes 2359552 | tf_op jit(solution)/shard_map/while/body/eval_jaxpr/gather | solution.py:14
  65.0 0.7 dynamic-slice_bitcast_fusion.2
  67.0 1.1 constant_dynamic-slice_fusion.3
  68.6 1.2 fusion.33
  70.1 0.9 convolution_convert_fusion.2
  71.5 0.7 fusion.32
  72.2 3.4 %gather_fusion = bf16[64,16,576]{2,1,0:T(8,128)(2,1)S(1)} fusion(bf16[272,16,576]{2,1,0:T(8,128)(2,1)} %get-tuple-element.201, s32[1024]{0:T(1024)S(1)} %pad_clamp_fusion.3), kind=kCustom, calls=%fused_computation.clone.1 | custom fusion | bytes 2359552 | tf_op jit(solution)/shard_map/while/body/eval_jaxpr/gather | solution.py:14
  75.7 0.7 dynamic-slice_bitcast_fusion.2
  77.6 1.1 constant_dynamic-slice_fusion.3
  79.2 1.2 fusion.33
  80.8 0.9 convolution_convert_fusion.2
  82.9 3.4 %gather_fusion = bf16[64,16,576]{2,1,0:T(8,128)(2,1)S(1)} fusion(bf16[272,16,576]{2,1,0:T(8,128)(2,1)} %get-tuple-element.201, s32[1024]{0:T(1024)S(1)} %pad_clamp_fusion.3), kind=kCustom, calls=%fused_computation.clone.1 | custom fusion | bytes 2359552 | tf_op jit(solution)/shard_map/while/body/eval_jaxpr/gather | solution.py:14
  86.3 0.7 dynamic-slice_bitcast_fusion.2
  88.2 1.1 constant_dynamic-slice_fusion.3
  89.8 1.2 fusion.33
  91.4 0.9 convolution_convert_fusion.2
  92.8 53.2 %all-gather.2.cloned.1.call-done = bf16[128,512,128]{2,1,0:T(8,128)(2,1)} async-done(((bf16[8,512,128]{2,1,0:T(8,128)(2,1)}), bf16[128,512,128]{2,1,0:T(8,128)(2,1)}) %all-gather.2.cloned.1.call-update) | async-done | bytes 16777232 | tf_op jit(solution)/shard_map/all_gather | solution.py:56
  146.1 7.3 %fusion.22 = bf16[128,4,1,4,128]{4,3,2,1,0:T(4,128)(2,1)S(1)} fusion(bf16[4,4,128,512]{3,1,0,2:T(4,128)(2,1)S(1)} %get-tuple-element.96, bf16[128,512,128]{2,1,0:T(8,128)(2,1)} %all-gather.2.cloned.1.call-done), kind=kOutput, calls=%fused_computation.40 | convolution fusion | flops 268697600 | bytes 19398656 | tf_op jit(solution)/shard_map/rjhc,hcv->rjhv/dot_general | solution.py:53
  153.4 1.0 copy.34
  (44 shorter events, 12.3 us)
Async XLA Ops:
  6.5 139.5 %all-gather.2.cloned.1.call-start = ((), (), s32[]{:S(2)}) async-start(), calls=%async_computation.1 | async-start | bytes 17825792 | tf_op jit(solution)/shard_map/all_gather | solution.py:56
  7.3 9.0 %copy-start = (s32[1,16]{1,0:T(1,128)S(1)}, s32[1,16]{1,0:T(1,128)}, u32[]{:S(2)}) copy-start(s32[1,16]{1,0:T(1,128)} %param.12) | copy-start | bytes 196
  20.2 24.4 %all-to-all-start = ((bf16[16,16,576]{2,1,0:T(8,128)(2,1)}), bf16[16,16,576]{2,1,0:T(8,128)(2,1)S(1)}, u32[]{:S(2)}, u32[]{:S(2)}) async-start(bf16[16,16,576]{2,1,0:T(8,128)(2,1)} %broadcast_select_fusion), calls=%async_computation | async-start | bytes 655360 | tf_op jit(solution)/shard_map/all_to_all | solution.py:46
  27.9 22.4 %copy-start.1 = (s32[4]{0:T(128)S(1)}, s32[4]{0:T(128)}, u32[]{:S(2)}) copy-start(s32[4]{0:T(128)} %param.14) | copy-start | bytes 52
Sparse Core Ops, SparseCore 0:
  9.5 136.4 all-gather.1
where the time goes:
time: 162 us; the launch traced here: 161 us
  waiting for transfers between devices  70.6 us (44%)
  local copies, waits for them, and re-layouts  39.9 us (25%)
  matrix products  15.8 us (10%)
  other arithmetic  13.5 us (8%)
  between operations  13.5 us (8%)
  starting transfers between devices  7.7 us (5%)
    all_gather x1, waiting for transfers between devices, per_device(): lax.all_gather(value_up_matrix, ('ep', 'sub'), axis=0, tiled=True)  53.2 us
    all_to_all x1, waiting for transfers between devices, per_device(): lax.all_to_all(outgoing, ('ep', 'sub'), split_axis=0, concat_axis=0, tile...  16.7 us
    gather x4, local copies, waits for them, and re-layouts, attend(): cache_keys = page_store[page_rows].reshape(-1, key_width)  13.6 us
    unnamed x5, local copies, waits for them, and re-layouts  8.97 us
    dynamic_slice x12, local copies, waits for them, and re-layouts, per_device(): lax.map(one_request, (queries, draft_keys, page_table, cache_length))  8.61 us
    all_to_all x1, starting transfers between devices, per_device(): lax.all_to_all(outgoing, ('ep', 'sub'), split_axis=0, concat_axis=0, tile...  7.7 us
    dot_general x1, matrix products, per_device(): jnp.einsum('rjhc,hcv->rjhv', latent_state, lax.all_gather(value_up_matrix...  7.35 us
    concatenate x1, other arithmetic, per_device(): page_store = jnp.concatenate([page_pool, received], axis=0)  5.73 us
  transfers between devices with their start and end apart: 2, of which 2 were waited for; matrix products, arithmetic and copies ran while one was open for 38% of the time, Pallas kernels for 0%

commit v1 on v0

v1 whole, which is shorter than its diff:
```python
import functools
import math

import jax
import jax.numpy as jnp
from jax import lax
from jax.experimental import pallas as pl
from jax.experimental.pallas import tpu as pltpu
from jax.sharding import PartitionSpec as P

LATENT_WIDTH = 512
AXES = ("ep", "sub")
EXP2_SCALE = 192 ** (-0.5) * math.log2(math.e)
DEAD = -1e30


def attend_kernel(length_ref, table_ref, query_ref, draft_ref, pool_ref, received_ref, latent_ref, keys, bias):
    request = pl.program_id(0)
    requests, rows, width = keys.shape
    page, _, pool_pages = pool_ref.shape
    peers = received_ref.shape[1]
    draft = draft_ref.shape[1]
    heads = query_ref.shape[3]
    pages = table_ref.shape[0] // requests
    context = pages * page

    @pl.when(request == 0)
    def _():
        table = table_ref[...]
        column = lax.broadcasted_iota(jnp.int32, (requests * pages, pool_pages), 1)
        pick_own = jnp.where(column == table, 1.0, 0.0).astype(jnp.bfloat16)
        column = lax.broadcasted_iota(jnp.int32, (requests * pages, peers), 1)
        pick_received = jnp.where(column + pool_pages == table, 1.0, 0.0).astype(jnp.bfloat16)
        for place in range(page):
            got = lax.dot_general(
                pick_own, pool_ref[place], (((1,), (1,)), ((), ())), preferred_element_type=jnp.float32
            ) + jnp.dot(pick_received, received_ref[place], preferred_element_type=jnp.float32)
            keys[:, place * pages : (place + 1) * pages, :] = got.astype(jnp.bfloat16).reshape(
                requests, pages, width
            )
        for r in range(requests):
            keys[r, context:rows, :] = jnp.concatenate(
                [draft_ref[r].astype(jnp.float32), jnp.zeros((rows - context - draft, width), jnp.float32)], axis=0
            ).astype(jnp.bfloat16)

    row = lax.broadcasted_iota(jnp.int32, (context, heads), 0)
    position = lax.rem(row, pages) * page + lax.div(row, pages)
    bias[...] = jnp.where(position < length_ref[request], 0.0, DEAD)
    late = lax.broadcasted_iota(jnp.int32, (rows - context, heads), 0)
    for pair in range(0, draft, 2):
        query = jnp.concatenate([query_ref[0, pair], query_ref[0, pair + 1]], axis=1)
        scores = jnp.dot(keys[request], query, preferred_element_type=jnp.float32)
        weights = []
        for j in range(2):
            part = scores[:, j * heads : (j + 1) * heads]
            early = part[:context] + bias[...]
            own = jnp.where(late <= pair + j, part[context:], DEAD)
            top = jnp.maximum(
                jnp.max(early, axis=0, keepdims=True), jnp.max(own, axis=0, keepdims=True)
            )
            early = jnp.exp2((early - top) * EXP2_SCALE)
            own = jnp.exp2((own - top) * EXP2_SCALE)
            total = jnp.sum(early, axis=0, keepdims=True) + jnp.sum(own, axis=0, keepdims=True)
            inverse = 1.0 / total
            weights.append(
                jnp.concatenate(
                    [(early * inverse).astype(jnp.bfloat16), (own * inverse).astype(jnp.bfloat16)], axis=0
                )
            )
        latent = lax.dot_general(
            jnp.concatenate(weights, axis=1),
            keys[request, :, :LATENT_WIDTH],
            (((0,), (0,)), ((), ())),
            preferred_element_type=jnp.float32,
        ).astype(jnp.bfloat16)
        latent_ref[0, pair] = latent[:heads]
        latent_ref[0, pair + 1] = latent[heads:]


def per_device(
    queries, draft_keys, page_pool, send_slot, page_table, cache_length, value_up_matrix
):
    requests, draft, heads, width = queries.shape
    pool_pages, page, _ = page_pool.shape
    peers = send_slot.shape[1]
    pages = page_table.shape[1]
    choose = (send_slot[0][:, None] == jnp.arange(pool_pages, dtype=jnp.int32)[None, :]).astype(jnp.bfloat16)
    outgoing = jnp.einsum("qp,psk->qsk", choose, page_pool, preferred_element_type=jnp.bfloat16)
    received = lax.all_to_all(outgoing, AXES, split_axis=0, concat_axis=0, tiled=True)
    received = received.transpose(1, 0, 2)
    rows = pages * page + 16
    vmem = pl.BlockSpec(memory_space=pltpu.VMEM)
    latent = pl.pallas_call(
        attend_kernel,
        grid=(requests,),
        out_shape=jax.ShapeDtypeStruct((requests, draft, heads, LATENT_WIDTH), jnp.bfloat16),
        in_specs=[
            pl.BlockSpec(memory_space=pltpu.SMEM),
            vmem,
            pl.BlockSpec((1, draft, width, heads), lambda r: (r, 0, 0, 0)),
            vmem,
            vmem,
            vmem,
        ],
        out_specs=pl.BlockSpec((1, draft, heads, LATENT_WIDTH), lambda r: (r, 0, 0, 0)),
        scratch_shapes=[
            pltpu.VMEM((requests, rows, width), jnp.bfloat16),
            pltpu.VMEM((pages * page, heads), jnp.float32),
        ],
        compiler_params=pltpu.CompilerParams(vmem_limit_bytes=48 * 2**20),
        name="attend",
    )(
        cache_length,
        page_table.reshape(-1, 1),
        queries.swapaxes(2, 3),
        draft_keys,
        page_pool.transpose(1, 2, 0),
        received,
    )
    shares = lax.all_to_all(
        latent.reshape(requests * draft, heads, LATENT_WIDTH), AXES, split_axis=1, concat_axis=0, tiled=True
    )
    mixed = jnp.einsum(
        "rhc,hcv->rhv", shares, value_up_matrix, preferred_element_type=jnp.float32
    ).astype(jnp.bfloat16)
    mixed = lax.all_to_all(mixed, AXES, split_axis=0, concat_axis=1, tiled=True)
    return mixed.reshape(requests, draft, -1)


def solution(mesh):
    placed = (
        P(("groups", "ep", "sub"), None, None, None),
        P(("groups", "ep", "sub"), None, None),
        P(("groups", "ep", "sub"), None, None),
        P(("groups", "ep", "sub"), None),
        P(("groups", "ep", "sub"), None),
        P(("groups", "ep", "sub")),
        P(("ep", "sub"), None, None),
    )
    return jax.shard_map(
        per_device,
        mesh=mesh,
        in_specs=placed,
        out_specs=P(("groups", "ep", "sub"), None, None),
        check_vma=False,
    )
```

time: 162 us -> 121 us (0.75)
  blocking collectives: 0 us -> 69.7 us
  waiting for transfers between devices: 70.6 us -> 11 us
  local copies, waits for them, and re-layouts: 39.9 us -> 5.52 us
  Pallas kernels: 0 us -> 21.9 us
  other arithmetic: 13.5 us -> 0 us
  between operations: 13.5 us -> 0.11 us
  matrix products: 15.8 us -> 4.59 us
    all_to_all x0 -> x2, blocking collectives: none -> 69.7 us  [the longest x1 50.4 us: per_device(): lax.all_to_all(latent.reshape(requests * draft, heads, LATENT_WIDTH), AXE...]
    all_gather x1 -> x0, waiting for transfers between devices: 53.2 us -> none  [per_device(): lax.all_gather(value_up_matrix, ('ep', 'sub'), axis=0, tiled=True)]
    pallas_call x0 -> x1, Pallas kernels: none -> 21.9 us  [per_device(): pl.pallas_call(attend_kernel, grid=(requests,), out_shape=jax.ShapeDtypeS...]
    gather x5 -> x0, local copies, waits for them, and re-layouts: 16.7 us -> none  [the longest x4 13.6 us: attend(): cache_keys = page_store[page_rows].reshape(-1, key_width)]
    dot_general x9 -> x2, matrix products: 15.8 us -> 4.59 us  [the longest x1 3.9 us: per_device(): jnp.einsum('qp,psk->qsk', choose, page_pool, preferred_element_type=jnp.b...]
    dynamic_slice x12 -> x0, local copies, waits for them, and re-layouts: 8.61 us -> none  [per_device(): lax.map(one_request, (queries, draft_keys, page_table, cache_length))]
    unnamed x5 -> x10, local copies, waits for them, and re-layouts: 8.97 us -> 0.74 us
    concatenate x1 -> x0, other arithmetic: 5.73 us -> none  [per_device(): page_store = jnp.concatenate([page_pool, received], axis=0)]
  transfers between devices with their start and end apart: 2 -> 1, of which waited for: 2 -> 1; matrix products, arithmetic and copies ran while one was open for 38% -> 0% of each run, Pallas kernels for 0% -> 0%
where the time goes in v1:
time: 121 us; the launch traced here: 120 us
  blocking collectives  69.7 us (58%)
  Pallas kernels  21.9 us (18%)
  waiting for transfers between devices  11 us (9%)
  starting transfers between devices  7.41 us (6%)
  local copies, waits for them, and re-layouts  5.52 us (5%)
  matrix products  4.59 us (4%)
    all_to_all x1, blocking collectives, per_device(): lax.all_to_all(latent.reshape(requests * draft, heads, LATENT_WIDTH), AXE...  50.4 us
    pallas_call x1, Pallas kernels, per_device(): pl.pallas_call(attend_kernel, grid=(requests,), out_shape=jax.ShapeDtypeS...  21.9 us
    all_to_all x1, blocking collectives, per_device(): mixed = lax.all_to_all(mixed, AXES, split_axis=0, concat_axis=1, tiled=True)  19.4 us
    all_to_all x1, waiting for transfers between devices, per_device(): lax.all_to_all(outgoing, AXES, split_axis=0, concat_axis=0, tiled=True)  11 us
    all_to_all x1, starting transfers between devices, per_device(): lax.all_to_all(outgoing, AXES, split_axis=0, concat_axis=0, tiled=True)  7.41 us
    dot_general x1, matrix products, per_device(): jnp.einsum('qp,psk->qsk', choose, page_pool, preferred_element_type=jnp.b...  3.9 us
  transfers between devices with their start and end apart: 1, of which 1 were waited for; matrix products, arithmetic and copies ran while one was open for 0% of the time, Pallas kernels for 0%

profile of v1, /device:TPU:0, one launch (start us, length us, event | category | flops | bytes accessed | tf_op | source)
XLA Modules:
  0.0 120.2 jit_solution(11966396725062904226)
XLA Ops:
  0.0 0.0 copy-start
  0.0 0.0 copy-start.4
  0.0 0.0 copy-start.1
  0.0 3.9 %fusion.2 = bf16[16,16,576]{2,0,1:T(8,128)(2,1)S(1)} fusion(bf16[256,16,576]{0,2,1:T(8,128)(2,1)} %param.9, s32[16]{0:T(128)} %bitcast.31), kind=kOutput, calls=%fused_computation.5 | convolution fusion | flops 75501568 | bytes 5013568 | tf_op jit(solution)/shard_map/qp,psk->qsk/dot_general | solution.py:88
  3.9 0.0 copy-start.3
  3.9 0.8 copy.13
  4.7 7.4 %all-to-all-start = ((bf16[16,16,576]{2,1,0:T(8,128)(2,1)}), bf16[16,16,576]{2,1,0:T(8,128)(2,1)}, u32[]{:S(2)}, u32[]{:S(2)}) async-start(bf16[16,16,576]{2,1,0:T(8,128)(2,1)} %copy.13), calls=%async_computation | async-start | bytes 655360 | tf_op jit(solution)/shard_map/all_to_all | solution.py:89
  12.1 0.0 copy-done.4
  12.1 0.1 reshape.15.table_ref
  12.3 11.0 %all-to-all-done = bf16[16,16,576]{2,1,0:T(8,128)(2,1)} async-done(((bf16[16,16,576]{2,1,0:T(8,128)(2,1)}), bf16[16,16,576]{2,1,0:T(8,128)(2,1)}, u32[]{:S(2)}, u32[]{:S(2)}) %all-to-all-start) | async-done | bytes 294944 | tf_op jit(solution)/shard_map/all_to_all | solution.py:89
  23.3 1.0 copy.21
  24.3 0.0 copy-done.1
  24.3 0.0 copy-done.3
  24.3 0.0 copy-start.2
  24.3 0.7 copy-done.2
  25.1 21.9 %attend.1 = bf16[4,4,128,512]{3,2,1,0:T(8,128)(2,1)S(1)} custom-call(s32[4]{0:T(128)S(1)} %copy-done.3, s32[256,1]{1,0:T(8,128)S(1)} %reshape.15.table_ref, bf16[4,4,576,128]{3,2,1,0:T(8,128)(2,1)S(1)} %bitcast.25, bf16[4,4,576]{2,1,0:T(4,128)(2,1)S(1)} %copy-done.2, bf16[16,576,256]{2,1,0:T(8,128)(2,1)} %bitcast.27, bf16[16,16,576]{2,1,0:T(8,128)(2,1)S(1)} %bitcast.26), custom_call_target="tpu_custom_call" | custom-call | tf_op jit(solution)/shard_map/attend/pallas_call | solution.py:93
  46.9 1.2 copy.16
  48.1 50.4 %all_to_all.38 = bf16[16,128,512]{2,0,1:T(8,128)(2,1)S(1)} all-to-all(bf16[16,128,512]{2,0,1:T(8,128)(2,1)S(1)} %copy.16), channel_id=1, replica_groups=mesh['groups'=2,'ep'=8,'sub'=2] {'ep','sub'}, dimensions={1} | all-to-all | bytes 4194304 | tf_op jit(solution)/shard_map/all_to_all | solution.py:120
  98.5 0.2 copy.17
  98.7 0.0 copy-done
  98.7 0.7 fusion
  99.4 0.3 copy.18
  99.8 19.4 %all_to_all.39 = bf16[256,8,128]{2,1,0:T(8,128)(2,1)S(1)} all-to-all(bf16[256,8,128]{2,1,0:T(8,128)(2,1)S(1)} %copy.18), channel_id=1, replica_groups=mesh['groups'=2,'ep'=8,'sub'=2] {'ep','sub'}, dimensions={0} | all-to-all | bytes 1048576 | tf_op jit(solution)/shard_map/all_to_all | solution.py:126
  119.2 0.1 copy.19
  119.3 1.0 reshape.13
Async XLA Ops:
  0.0 98.7 %copy-start = (bf16[8,512,128]{2,1,0:T(8,128)(2,1)S(1)}, bf16[8,512,128]{2,1,0:T(8,128)(2,1)}, u32[]{:S(2)}) copy-start(bf16[8,512,128]{2,1,0:T(8,128)(2,1)} %param.13) | copy-start | bytes 3145732
  0.0 12.1 %copy-start.4 = (s32[4,64]{1,0:T(4,128)S(1)}, s32[4,64]{1,0:T(4,128)}, u32[]{:S(2)}) copy-start(s32[4,64]{1,0:T(4,128)} %param.11) | copy-start | bytes 3076
  0.0 24.3 %copy-start.1 = (bf16[4,4,128,576]{2,3,1,0:T(8,128)(2,1)S(1)}, bf16[4,4,128,576]{2,3,1,0:T(8,128)(2,1)}, u32[]{:S(2)}) copy-start(bf16[4,4,128,576]{2,3,1,0:T(8,128)(2,1)} %param.7) | copy-start | bytes 7077892
  3.9 20.4 %copy-start.3 = (s32[4]{0:T(128)S(1)}, s32[4]{0:T(128)}, u32[]{:S(2)}) copy-start(s32[4]{0:T(128)} %length_ref.1) | copy-start | bytes 52
  4.7 18.6 %all-to-all-start = ((bf16[16,16,576]{2,1,0:T(8,128)(2,1)}), bf16[16,16,576]{2,1,0:T(8,128)(2,1)}, u32[]{:S(2)}, u32[]{:S(2)}) async-start(bf16[16,16,576]{2,1,0:T(8,128)(2,1)} %copy.13), calls=%async_computation | async-start | bytes 655360 | tf_op jit(solution)/shard_map/all_to_all | solution.py:89
  24.3 0.7 copy-start.2

commit v2 on v0

v2 whole, which is shorter than its diff:
```python
import functools
import math

import jax
import jax.numpy as jnp
from jax import lax
from jax.experimental import pallas as pl
from jax.experimental.pallas import tpu as pltpu
from jax.sharding import PartitionSpec as P

LATENT_WIDTH = 512
AXES = ("ep", "sub")
EXP2_SCALE = 192 ** (-0.5) * math.log2(math.e)
DEAD = -1e30


def exchange_kernel(
    groups_of,
    length_ref,
    table_ref,
    query_ref,
    draft_ref,
    pool_ref,
    outgoing_ref,
    matrix_ref,
    back_ref,
    keys,
    bias,
    arrived_pages,
    matrix,
    sending,
    arrived,
    mixed,
    page_sent,
    page_got,
    latent_sent,
    latent_got,
    mixed_sent,
    mixed_got,
):
    requests, rows, width = keys.shape
    page, _, pool_pages = pool_ref.shape
    peers = outgoing_ref.shape[0]
    draft = draft_ref.shape[1]
    heads = query_ref.shape[3]
    pages = table_ref.shape[0] // requests
    context = pages * page
    own_heads, latent_width, value_width = matrix_ref.shape
    outer, inner = groups_of
    me = lax.axis_index("ep") * inner + lax.axis_index("sub")

    def place_of(peer):
        return {"ep": lax.div(peer, inner), "sub": lax.rem(peer, inner)}

    def copy_to(source, target, sent, got, peer):
        return pltpu.make_async_remote_copy(
            src_ref=source,
            dst_ref=target,
            send_sem=sent,
            recv_sem=got,
            device_id=place_of(peer),
            device_id_type=pl.DeviceIdType.MESH,
        )

    barrier = pltpu.get_barrier_semaphore()

    @pl.loop(1, peers)
    def _(step):
        pl.semaphore_signal(
            barrier,
            inc=1,
            device_id=place_of(lax.rem(me + step, peers)),
            device_id_type=pl.DeviceIdType.MESH,
        )

    pl.semaphore_wait(barrier, peers - 1)

    @pl.loop(1, peers)
    def _(step):
        peer = lax.rem(me + step, peers)
        copy_to(outgoing_ref.at[peer], arrived_pages.at[me], page_sent, page_got, peer).start()

    arrived_pages[me] = outgoing_ref[me]
    for h in range(own_heads):
        matrix[:, h * value_width : (h + 1) * value_width] = matrix_ref[h]

    table = table_ref[...]
    column = lax.broadcasted_iota(jnp.int32, (requests * pages, pool_pages), 1)
    pick_own = jnp.where(column == table, 1.0, 0.0).astype(jnp.bfloat16)

    @pl.loop(0, page)
    def _(place):
        got = lax.dot_general(
            pick_own, pool_ref[place], (((1,), (1,)), ((), ())), preferred_element_type=jnp.float32
        ).astype(jnp.bfloat16)
        start = pl.multiple_of(place * pages, pages)
        keys[:, pl.ds(start, pages), :] = got.reshape(requests, pages, width)

    for r in range(requests):
        keys[r, context:rows, :] = jnp.concatenate(
            [draft_ref[r].astype(jnp.float32), jnp.zeros((rows - context - draft, width), jnp.float32)], axis=0
        ).astype(jnp.bfloat16)

    all_pages = pl.ds(0, peers - 1)
    copy_to(outgoing_ref.at[all_pages], arrived_pages.at[all_pages], page_sent, page_got, me).wait_recv()
    column = lax.broadcasted_iota(jnp.int32, (requests * pages, peers * page), 1)
    page_match = lax.div(column, page) + pool_pages == table
    column_place = lax.rem(column, page)
    received = arrived_pages[...].reshape(peers * page, width)

    @pl.loop(0, page)
    def _(place):
        pick = jnp.where(page_match & (column_place == place), 1.0, 0.0).astype(jnp.bfloat16)
        got = jnp.dot(pick, received, preferred_element_type=jnp.float32).astype(jnp.bfloat16)
        start = pl.multiple_of(place * pages, pages)
        keys[:, pl.ds(start, pages), :] += got.reshape(requests, pages, width)

    @pl.loop(0, requests)
    def _(request):
        row = lax.broadcasted_iota(jnp.int32, (context, heads), 0)
        position = lax.rem(row, pages) * page + lax.div(row, pages)
        bias[...] = jnp.where(position < length_ref[request], 0.0, DEAD)
        late = lax.broadcasted_iota(jnp.int32, (rows - context, heads), 0)
        for pair in range(0, draft, 2):
            query = jnp.concatenate([query_ref[request, pair], query_ref[request, pair + 1]], axis=1)
            scores = jnp.dot(keys[request], query, preferred_element_type=jnp.float32)
            weights = []
            for j in range(2):
                part = scores[:, j * heads : (j + 1) * heads]
                early = part[:context] + bias[...]
                own = jnp.where(late <= pair + j, part[context:], DEAD)
                top = jnp.maximum(
                    jnp.max(early, axis=0, keepdims=True), jnp.max(own, axis=0, keepdims=True)
                )
                early = jnp.exp2((early - top) * EXP2_SCALE)
                own = jnp.exp2((own - top) * EXP2_SCALE)
                total = jnp.sum(early, axis=0, keepdims=True) + jnp.sum(own, axis=0, keepdims=True)
                inverse = 1.0 / total
                weights.append(
                    jnp.concatenate(
                        [(early * inverse).astype(jnp.bfloat16), (own * inverse).astype(jnp.bfloat16)], axis=0
                    )
                )
            latent = lax.dot_general(
                jnp.concatenate(weights, axis=1),
                keys[request, :, :latent_width],
                (((0,), (0,)), ((), ())),
                preferred_element_type=jnp.float32,
            )
            for p in range(peers):
                first = p * own_heads
                both = jnp.concatenate(
                    [latent[first : first + own_heads], latent[heads + first : heads + first + own_heads]], axis=0
                )
                sending[request, p, pair * own_heads : (pair + 2) * own_heads, :] = both.astype(jnp.bfloat16)

        @pl.loop(1, peers)
        def _(step):
            peer = lax.rem(me + step, peers)
            copy_to(
                sending.at[request, peer],
                arrived.at[request, me],
                latent_sent.at[request],
                latent_got.at[request],
                peer,
            ).start()

        arrived[request, me] = sending[request, me]

    @pl.loop(0, requests)
    def _(request):
        copy_to(
            sending.at[request, all_pages],
            arrived.at[request, all_pages],
            latent_sent.at[request],
            latent_got.at[request],
            me,
        ).wait_recv()
        block = draft * own_heads
        every = jnp.dot(
            arrived[request].reshape(peers * block, latent_width), matrix[...], preferred_element_type=jnp.float32
        )
        head = lax.rem(lax.broadcasted_iota(jnp.int32, (peers * block, value_width), 0), own_heads)
        chosen = every[:, :value_width]
        for h in range(1, own_heads):
            chosen = jnp.where(head == h, every[:, h * value_width : (h + 1) * value_width], chosen)
        mixed[request] = chosen.astype(jnp.bfloat16).reshape(peers, block, value_width)

        @pl.loop(1, peers)
        def _(step):
            peer = lax.rem(me + step, peers)
            copy_to(
                mixed.at[request, peer],
                back_ref.at[request, me],
                mixed_sent.at[request],
                mixed_got.at[request],
                peer,
            ).start()

        back_ref[request, me] = mixed[request, me]

    copy_to(outgoing_ref.at[all_pages], arrived_pages.at[all_pages], page_sent, page_got, me).wait_send()

    @pl.loop(0, requests)
    def _(request):
        copy_to(
            sending.at[request, all_pages],
            arrived.at[request, all_pages],
            latent_sent.at[request],
            latent_got.at[request],
            me,
        ).wait_send()
        copy_to(
            mixed.at[request, all_pages],
            back_ref.at[request, all_pages],
            mixed_sent.at[request],
            mixed_got.at[request],
            me,
        ).wait()


def per_device(
    groups_of, queries, draft_keys, page_pool, send_slot, page_table, cache_length, value_up_matrix
):
    requests, draft, heads, width = queries.shape
    pool_pages, page, _ = page_pool.shape
    peers = send_slot.shape[1]
    pages = page_table.shape[1]
    own_heads, _, value_width = value_up_matrix.shape
    choose = (send_slot[0][:, None] == jnp.arange(pool_pages, dtype=jnp.int32)[None, :]).astype(jnp.bfloat16)
    outgoing = jnp.einsum("qp,psk->qsk", choose, page_pool, preferred_element_type=jnp.bfloat16)
    rows = pages * page + 16
    block = draft * own_heads
    vmem = pl.BlockSpec(memory_space=pltpu.VMEM)
    back = pl.pallas_call(
        functools.partial(exchange_kernel, groups_of),
        out_shape=jax.ShapeDtypeStruct((requests, peers, block, value_width), jnp.bfloat16),
        in_specs=[pl.BlockSpec(memory_space=pltpu.SMEM)] + [vmem] * 6,
        out_specs=vmem,
        scratch_shapes=[
            pltpu.VMEM((requests, rows, width), jnp.bfloat16),
            pltpu.VMEM((pages * page, heads), jnp.float32),
            pltpu.VMEM((peers, page, width), jnp.bfloat16),
            pltpu.VMEM((LATENT_WIDTH, own_heads * value_width), jnp.bfloat16),
            pltpu.VMEM((requests, peers, block, LATENT_WIDTH), jnp.bfloat16),
            pltpu.VMEM((requests, peers, block, LATENT_WIDTH), jnp.bfloat16),
            pltpu.VMEM((requests, peers, block, value_width), jnp.bfloat16),
            pltpu.SemaphoreType.DMA,
            pltpu.SemaphoreType.DMA,
            pltpu.SemaphoreType.DMA((requests,)),
            pltpu.SemaphoreType.DMA((requests,)),
            pltpu.SemaphoreType.DMA((requests,)),
            pltpu.SemaphoreType.DMA((requests,)),
        ],
        compiler_params=pltpu.CompilerParams(
            collective_id=0, has_side_effects=True, vmem_limit_bytes=48 * 2**20
        ),
        name="exchange",
    )(
        cache_length,
        page_table.reshape(-1, 1),
        queries.swapaxes(2, 3),
        draft_keys,
        page_pool.transpose(1, 2, 0),
        outgoing,
        value_up_matrix,
    )
    back = back.reshape(requests, peers, draft, own_heads * value_width)
    return back.swapaxes(1, 2).reshape(requests, draft, heads * value_width)


def solution(mesh):
    placed = (
        P(("groups", "ep", "sub"), None, None, None),
        P(("groups", "ep", "sub"), None, None),
        P(("groups", "ep", "sub"), None, None),
        P(("groups", "ep", "sub"), None),
        P(("groups", "ep", "sub"), None),
        P(("groups", "ep", "sub")),
        P(("ep", "sub"), None, None),
    )
    return jax.shard_map(
        functools.partial(per_device, (mesh.shape["ep"], mesh.shape["sub"])),
        mesh=mesh,
        in_specs=placed,
        out_specs=P(("groups", "ep", "sub"), None, None),
        check_vma=False,
    )
```

time: 162 us -> 89.3 us (0.55)
  Pallas kernels: 0 us -> 83.3 us
  waiting for transfers between devices: 70.6 us -> 0 us
  local copies, waits for them, and re-layouts: 39.9 us -> 1.97 us
  other arithmetic: 13.5 us -> 0 us
  between operations: 13.5 us -> 0.07 us
  matrix products: 15.8 us -> 3.84 us
  starting transfers between devices: 7.7 us -> 0 us
    pallas_call x0 -> x1, Pallas kernels: none -> 83.3 us  [per_device(): pl.pallas_call(functools.partial(exchange_kernel, groups_of), out_shape=j...]
    all_gather x1 -> x0, waiting for transfers between devices: 53.2 us -> none  [per_device(): lax.all_gather(value_up_matrix, ('ep', 'sub'), axis=0, tiled=True)]
    gather x5 -> x0, local copies, waits for them, and re-layouts: 16.7 us -> none  [the longest x4 13.6 us: attend(): cache_keys = page_store[page_rows].reshape(-1, key_width)]
    all_to_all x1 -> x0, waiting for transfers between devices: 16.7 us -> none  [per_device(): lax.all_to_all(outgoing, ('ep', 'sub'), split_axis=0, concat_axis=0, tile...]
    dot_general x9 -> x1, matrix products: 15.8 us -> 3.84 us  [per_device(): jnp.einsum('qp,psk->qsk', choose, page_pool, preferred_element_type=jnp.b...]
    unnamed x5 -> x8, local copies, waits for them, and re-layouts: 8.97 us -> 0.02 us
    dynamic_slice x12 -> x0, local copies, waits for them, and re-layouts: 8.61 us -> none  [per_device(): lax.map(one_request, (queries, draft_keys, page_table, cache_length))]
    all_to_all x1 -> x0, starting transfers between devices: 7.7 us -> none  [per_device(): lax.all_to_all(outgoing, ('ep', 'sub'), split_axis=0, concat_axis=0, tile...]
  transfers between devices with their start and end apart: 2 -> 0, of which waited for: 2 -> 0; matrix products, arithmetic and copies ran while one was open for 38% -> 0% of each run, Pallas kernels for 0% -> 0%
where the time goes in v2:
time: 89.3 us; the launch traced here: 89.1 us
  Pallas kernels  83.3 us (93%)
  matrix products  3.84 us (4%)
  local copies, waits for them, and re-layouts  1.97 us (2%)
    pallas_call x1, Pallas kernels, per_device(): pl.pallas_call(functools.partial(exchange_kernel, groups_of), out_shape=j...  83.3 us
    dot_general x1, matrix products, per_device(): jnp.einsum('qp,psk->qsk', choose, page_pool, preferred_element_type=jnp.b...  3.84 us

profile of v2, /device:TPU:0, one launch (start us, length us, event | category | flops | bytes accessed | tf_op | source)
XLA Modules:
  0.0 89.1 jit_solution(9912834103407999382)
XLA Ops:
  0.0 0.0 copy-start.3
  0.0 0.0 copy-start.2
  0.0 0.0 copy-start
  0.0 1.0 %reshape.14.table_ref = s32[256,1]{1,0:T(8,128)S(1)} reshape(s32[4,64]{1,0:T(4,128)} %param.11) | data formatting | bytes 2048 | tf_op jit(solution)/shard_map/reshape | solution.py:261
  1.0 0.0 copy-start.1
  1.0 3.8 %fusion.1 = bf16[16,16,576]{2,0,1:T(8,128)(2,1)S(1)} fusion(bf16[256,16,576]{0,2,1:T(8,128)(2,1)} %param.9, s32[16]{0:T(128)} %bitcast.14), kind=kOutput, calls=%fused_computation.2 | convolution fusion | flops 75501568 | bytes 5013568 | tf_op jit(solution)/shard_map/qp,psk->qsk/dot_general | solution.py:231
  4.8 0.1 copy.11.outgoing_ref
  4.9 0.0 copy-done.3
  4.9 0.0 copy-done.2
  4.9 0.0 copy-done
  4.9 0.0 copy-done.1
  5.0 83.3 %exchange.1 = bf16[4,16,32,128]{3,2,1,0:T(8,128)(2,1)S(1)} custom-call(s32[4]{0:T(128)S(1)} %copy-done.3, s32[256,1]{1,0:T(8,128)S(1)} %reshape.14.table_ref, bf16[4,4,576,128]{3,2,1,0:T(8,128)(2,1)S(1)} %bitcast.12, bf16[4,4,576]{2,1,0:T(4,128)(2,1)S(1)} %copy-done.2, bf16[16,576,256]{2,1,0:T(8,128)(2,1)} %bitcast.13, ...), custom_call_target="tpu_custom_call" | custom-call | tf_op jit(solution)/shard_map/exchange/pallas_call | solution.py:235
  88.2 0.9 %reshape.11 = bf16[4,16,4,1024]{3,2,1,0:T(4,128)(2,1)} reshape(bf16[4,16,32,128]{3,2,1,0:T(8,128)(2,1)S(1)} %exchange.1) | data formatting | bytes 1048576 | tf_op jit(solution)/shard_map/reshape | solution.py:268
Async XLA Ops:
  0.0 4.9 %copy-start.3 = (s32[4]{0:T(128)S(1)}, s32[4]{0:T(128)}, u32[]{:S(2)}) copy-start(s32[4]{0:T(128)} %length_ref.1) | copy-start | bytes 52
  0.0 4.9 %copy-start.2 = (bf16[4,4,576]{2,1,0:T(4,128)(2,1)S(1)}, bf16[4,4,576]{2,1,0:T(4,128)(2,1)}, u32[]{:S(2)}) copy-start(bf16[4,4,576]{2,1,0:T(4,128)(2,1)} %draft_ref.1) | copy-start | bytes 55300
  0.0 4.9 %copy-start = (bf16[4,4,128,576]{2,3,1,0:T(8,128)(2,1)S(1)}, bf16[4,4,128,576]{2,3,1,0:T(8,128)(2,1)}, u32[]{:S(2)}) copy-start(bf16[4,4,128,576]{2,3,1,0:T(8,128)(2,1)} %param.7) | copy-start | bytes 7077892
  1.0 4.0 %copy-start.1 = (bf16[8,512,128]{2,1,0:T(8,128)(2,1)S(1)}, bf16[8,512,128]{2,1,0:T(8,128)(2,1)}, u32[]{:S(2)}) copy-start(bf16[8,512,128]{2,1,0:T(8,128)(2,1)} %matrix_ref.1) | copy-start | bytes 3145732

commit v3 on v2

--- a/solution.py
+++ b/solution.py
@@ -37,6 +37,11 @@
     latent_got,
     mixed_sent,
     mixed_got,
+    far_matrix,
+    weights_sent,
+    weights_got,
+    swap_sent,
+    swap_got,
 ):
     requests, rows, width = keys.shape
     page, _, pool_pages = pool_ref.shape
@@ -46,8 +51,13 @@
     pages = table_ref.shape[0] // requests
     context = pages * page
     own_heads, latent_width, value_width = matrix_ref.shape
-    outer, inner = groups_of
+    groups, outer, inner = groups_of
     me = lax.axis_index("ep") * inner + lax.axis_index("sub")
+    near = peers // 2
+    side = lax.div(me, near)
+    seat = lax.rem(me, near)
+    group = lax.axis_index("groups")
+    share = latent_width // groups
 
     def place_of(peer):
         return {"ep": lax.div(peer, inner), "sub": lax.rem(peer, inner)}
@@ -73,16 +83,45 @@
             device_id_type=pl.DeviceIdType.MESH,
         )
 
-    pl.semaphore_wait(barrier, peers - 1)
+    for step in range(1, groups):
+        pl.semaphore_signal(
+            barrier,
+            inc=1,
+            device_id={"groups": lax.rem(group + step, groups)},
+            device_id_type=pl.DeviceIdType.MESH,
+        )
+    pl.semaphore_wait(barrier, peers + groups - 2)
 
     @pl.loop(1, peers)
     def _(step):
         peer = lax.rem(me + step, peers)
         copy_to(outgoing_ref.at[peer], arrived_pages.at[me], page_sent, page_got, peer).start()
 
+    own_share = pl.ds(pl.multiple_of(group * share, share), share)
+    across = pltpu.make_async_remote_copy(
+        src_ref=matrix_ref.at[:, own_share],
+        dst_ref=far_matrix.at[:, own_share],
+        send_sem=weights_sent,
+        recv_sem=weights_got,
+        device_id={"ep": lax.rem(lax.axis_index("ep") + outer // 2, outer)},
+        device_id_type=pl.DeviceIdType.MESH,
+    )
+    across.start()
+    swaps = [
+        pltpu.make_async_remote_copy(
+            src_ref=far_matrix.at[:, own_share],
+            dst_ref=far_matrix.at[:, own_share],
+            send_sem=swap_sent.at[step],
+            recv_sem=swap_got.at[step],
+            device_id={"groups": lax.rem(group + step, groups)},
+            device_id_type=pl.DeviceIdType.MESH,
+        )
+        for step in range(1, groups)
+    ]
+
     arrived_pages[me] = outgoing_ref[me]
     for h in range(own_heads):
-        matrix[:, h * value_width : (h + 1) * value_width] = matrix_ref[h]
+        matrix[side, :, h * value_width : (h + 1) * value_width] = matrix_ref[h]
 
     table = table_ref[...]
     column = lax.broadcasted_iota(jnp.int32, (requests * pages, pool_pages), 1)
@@ -154,65 +193,89 @@
                 )
                 sending[request, p, pair * own_heads : (pair + 2) * own_heads, :] = both.astype(jnp.bfloat16)
 
-        @pl.loop(1, peers)
+        @pl.loop(1, near)
         def _(step):
-            peer = lax.rem(me + step, peers)
-            copy_to(
-                sending.at[request, peer],
-                arrived.at[request, me],
-                latent_sent.at[request],
-                latent_got.at[request],
-                peer,
-            ).start()
-
-        arrived[request, me] = sending[request, me]
+            other = lax.rem(seat + step, near)
+            for half in range(2):
+                copy_to(
+                    sending.at[request, half * near + other],
+                    arrived.at[request, half * near + seat],
+                    latent_sent.at[request],
+                    latent_got.at[request],
+                    side * near + other,
+                ).start()
+
+        for half in range(2):
+            arrived[request, half * near + seat] = sending[request, half * near + seat]
+
+        @pl.when(request == max(requests - 2, 0))
+        def _():
+            across.wait_recv()
+            for swap in swaps:
+                swap.start()
+
+    for swap in swaps:
+        swap.wait_recv()
+    for h in range(own_heads):
+        matrix[1 - side, :, h * value_width : (h + 1) * value_width] = far_matrix[h]
+    near_pages = pl.ds(0, 2 * near - 2)
 
     @pl.loop(0, requests)
     def _(request):
         copy_to(
-            sending.at[request, all_pages],
-            arrived.at[request, all_pages],
+            sending.at[request, near_pages],
+            arrived.at[request, near_pages],
             latent_sent.at[request],
             latent_got.at[request],
             me,
         ).wait_recv()
         block = draft * own_heads
-        every = jnp.dot(
-            arrived[request].reshape(peers * block, latent_width), matrix[...], preferred_element_type=jnp.float32
-        )
-        head = lax.rem(lax.broadcasted_iota(jnp.int32, (peers * block, value_width), 0), own_heads)
-        chosen = every[:, :value_width]
-        for h in range(1, own_heads):
-            chosen = jnp.where(head == h, every[:, h * value_width : (h + 1) * value_width], chosen)
-        mixed[request] = chosen.astype(jnp.bfloat16).reshape(peers, block, value_width)
-
-        @pl.loop(1, peers)
+        head = lax.rem(lax.broadcasted_iota(jnp.int32, (near * block, value_width), 0), own_heads)
+        for half in range(2):
+            every = jnp.dot(
+                arrived[request, half * near : (half + 1) * near].reshape(near * block, latent_width),
+                matrix[half],
+                preferred_element_type=jnp.float32,
+            )
+            chosen = every[:, :value_width]
+            for h in range(1, own_heads):
+                chosen = jnp.where(head == h, every[:, h * value_width : (h + 1) * value_width], chosen)
+            mixed[request, half * near : (half + 1) * near] = chosen.astype(jnp.bfloat16).reshape(
+                near, block, value_width
+            )
+
+        @pl.loop(1, near)
         def _(step):
-            peer = lax.rem(me + step, peers)
-            copy_to(
-                mixed.at[request, peer],
-                back_ref.at[request, me],
-                mixed_sent.at[request],
-                mixed_got.at[request],
-                peer,
-            ).start()
-
-        back_ref[request, me] = mixed[request, me]
-
+            other = lax.rem(seat + step, near)
+            for half in range(2):
+                copy_to(
+                    mixed.at[request, half * near + other],
+                    back_ref.at[request, half * near + seat],
+                    mixed_sent.at[request],
+                    mixed_got.at[request],
+                    side * near + other,
+                ).start()
+
+        for half in range(2):
+            back_ref[request, half * near + seat] = mixed[request, half * near + seat]
+
+    across.wait_send()
+    for swap in swaps:
+        swap.wait_send()
     copy_to(outgoing_ref.at[all_pages], arrived_pages.at[all_pages], page_sent, page_got, me).wait_send()
 
     @pl.loop(0, requests)
     def _(request):
         copy_to(
-            sending.at[request, all_pages],
-            arrived.at[request, all_pages],
+            sending.at[request, near_pages],
+            arrived.at[request, near_pages],
             latent_sent.at[request],
             latent_got.at[request],
             me,
         ).wait_send()
         copy_to(
-            mixed.at[request, all_pages],
-            back_ref.at[request, all_pages],
+            mixed.at[request, near_pages],
+            back_ref.at[request, near_pages],
             mixed_sent.at[request],
             mixed_got.at[request],
             me,
@@ -241,7 +304,7 @@
             pltpu.VMEM((requests, rows, width), jnp.bfloat16),
             pltpu.VMEM((pages * page, heads), jnp.float32),
             pltpu.VMEM((peers, page, width), jnp.bfloat16),
-            pltpu.VMEM((LATENT_WIDTH, own_heads * value_width), jnp.bfloat16),
+            pltpu.VMEM((2, LATENT_WIDTH, own_heads * value_width), jnp.bfloat16),
             pltpu.VMEM((requests, peers, block, LATENT_WIDTH), jnp.bfloat16),
             pltpu.VMEM((requests, peers, block, LATENT_WIDTH), jnp.bfloat16),
             pltpu.VMEM((requests, peers, block, value_width), jnp.bfloat16),
@@ -251,6 +314,11 @@
             pltpu.SemaphoreType.DMA((requests,)),
             pltpu.SemaphoreType.DMA((requests,)),
             pltpu.SemaphoreType.DMA((requests,)),
+            pltpu.VMEM(value_up_matrix.shape, jnp.bfloat16),
+            pltpu.SemaphoreType.DMA,
+            pltpu.SemaphoreType.DMA,
+            pltpu.SemaphoreType.DMA((groups_of[0],)),
+            pltpu.SemaphoreType.DMA((groups_of[0],)),
         ],
         compiler_params=pltpu.CompilerParams(
             collective_id=0, has_side_effects=True, vmem_limit_bytes=48 * 2**20
@@ -280,7 +348,7 @@
         P(("ep", "sub"), None, None),
     )
     return jax.shard_map(
-        functools.partial(per_device, (mesh.shape["ep"], mesh.shape["sub"])),
+        functools.partial(per_device, (mesh.shape["groups"], mesh.shape["ep"], mesh.shape["sub"])),
         mesh=mesh,
         in_specs=placed,
         out_specs=P(("groups", "ep", "sub"), None, None),

time: 89.3 us -> 73.6 us (0.82)
  Pallas kernels: 83.3 us -> 67.6 us
    pallas_call x1, Pallas kernels: 83.3 us -> 67.6 us  [per_device(): pl.pallas_call(functools.partial(exchange_kernel, groups_of), out_shape=j...]
where the time goes in v3:
time: 73.6 us; the launch traced here: 73.4 us
  Pallas kernels  67.6 us (92%)
  matrix products  3.84 us (5%)
  local copies, waits for them, and re-layouts  1.97 us (3%)
    pallas_call x1, Pallas kernels, per_device(): pl.pallas_call(functools.partial(exchange_kernel, groups_of), out_shape=j...  67.6 us
    dot_general x1, matrix products, per_device(): jnp.einsum('qp,psk->qsk', choose, page_pool, preferred_element_type=jnp.b...  3.84 us

profile of v3, /device:TPU:0, one launch (start us, length us, event | category | flops | bytes accessed | tf_op | source)
XLA Modules:
  0.0 73.4 jit_solution(2621272037236138145)
XLA Ops:
  0.0 0.0 copy-start.3
  0.0 0.0 copy-start.2
  0.0 0.0 copy-start
  0.0 1.0 %reshape.14.table_ref = s32[256,1]{1,0:T(8,128)S(1)} reshape(s32[4,64]{1,0:T(4,128)} %param.11) | data formatting | bytes 2048 | tf_op jit(solution)/shard_map/reshape | solution.py:329
  1.0 0.0 copy-start.1
  1.0 3.8 %fusion.1 = bf16[16,16,576]{2,0,1:T(8,128)(2,1)S(1)} fusion(bf16[256,16,576]{0,2,1:T(8,128)(2,1)} %param.9, s32[16]{0:T(128)} %bitcast.14), kind=kOutput, calls=%fused_computation.2 | convolution fusion | flops 75501568 | bytes 5013568 | tf_op jit(solution)/shard_map/qp,psk->qsk/dot_general | solution.py:294
  4.8 0.1 copy.11.outgoing_ref
  4.9 0.0 copy-done.3
  4.9 0.0 copy-done.2
  4.9 0.0 copy-done
  4.9 0.0 copy-done.1
  5.0 67.6 %exchange.1 = bf16[4,16,32,128]{3,2,1,0:T(8,128)(2,1)S(1)} custom-call(s32[4]{0:T(128)S(1)} %copy-done.3, s32[256,1]{1,0:T(8,128)S(1)} %reshape.14.table_ref, bf16[4,4,576,128]{3,2,1,0:T(8,128)(2,1)S(1)} %bitcast.12, bf16[4,4,576]{2,1,0:T(4,128)(2,1)S(1)} %copy-done.2, bf16[16,576,256]{2,1,0:T(8,128)(2,1)} %bitcast.13, ...), custom_call_target="tpu_custom_call" | custom-call | tf_op jit(solution)/shard_map/exchange/pallas_call | solution.py:298
  72.5 0.9 %reshape.11 = bf16[4,16,4,1024]{3,2,1,0:T(4,128)(2,1)} reshape(bf16[4,16,32,128]{3,2,1,0:T(8,128)(2,1)S(1)} %exchange.1) | data formatting | bytes 1048576 | tf_op jit(solution)/shard_map/reshape | solution.py:336
Async XLA Ops:
  0.0 4.9 %copy-start.3 = (s32[4]{0:T(128)S(1)}, s32[4]{0:T(128)}, u32[]{:S(2)}) copy-start(s32[4]{0:T(128)} %length_ref.1) | copy-start | bytes 52
  0.0 4.9 %copy-start.2 = (bf16[4,4,576]{2,1,0:T(4,128)(2,1)S(1)}, bf16[4,4,576]{2,1,0:T(4,128)(2,1)}, u32[]{:S(2)}) copy-start(bf16[4,4,576]{2,1,0:T(4,128)(2,1)} %draft_ref.1) | copy-start | bytes 55300
  0.0 4.9 %copy-start = (bf16[4,4,128,576]{2,3,1,0:T(8,128)(2,1)S(1)}, bf16[4,4,128,576]{2,3,1,0:T(8,128)(2,1)}, u32[]{:S(2)}) copy-start(bf16[4,4,128,576]{2,3,1,0:T(8,128)(2,1)} %param.7) | copy-start | bytes 7077892
  1.0 4.0 %copy-start.1 = (bf16[8,512,128]{2,1,0:T(8,128)(2,1)S(1)}, bf16[8,512,128]{2,1,0:T(8,128)(2,1)}, u32[]{:S(2)}) copy-start(bf16[8,512,128]{2,1,0:T(8,128)(2,1)} %matrix_ref.1) | copy-start | bytes 3145732

commit v4 on v3

--- a/solution.py
+++ b/solution.py
@@ -208,17 +208,34 @@
         for half in range(2):
             arrived[request, half * near + seat] = sending[request, half * near + seat]
 
-        @pl.when(request == max(requests - 2, 0))
-        def _():
-            across.wait_recv()
-            for swap in swaps:
-                swap.start()
-
-    for swap in swaps:
-        swap.wait_recv()
-    for h in range(own_heads):
-        matrix[1 - side, :, h * value_width : (h + 1) * value_width] = far_matrix[h]
     near_pages = pl.ds(0, 2 * near - 2)
+    block = draft * own_heads
+
+    def raise_values(request, half):
+        seats = pl.ds(half * near, near)
+        every = jnp.dot(
+            arrived[request, seats].reshape(near * block, latent_width),
+            matrix[half],
+            preferred_element_type=jnp.float32,
+        )
+        head = lax.rem(lax.broadcasted_iota(jnp.int32, (near * block, value_width), 0), own_heads)
+        chosen = every[:, :value_width]
+        for h in range(1, own_heads):
+            chosen = jnp.where(head == h, every[:, h * value_width : (h + 1) * value_width], chosen)
+        mixed[request, seats] = chosen.astype(jnp.bfloat16).reshape(near, block, value_width)
+
+        @pl.loop(1, near)
+        def _(step):
+            other = lax.rem(seat + step, near)
+            copy_to(
+                mixed.at[request, half * near + other],
+                back_ref.at[request, half * near + seat],
+                mixed_sent.at[request],
+                mixed_got.at[request],
+                side * near + other,
+            ).start()
+
+        back_ref[request, half * near + seat] = mixed[request, half * near + seat]
 
     @pl.loop(0, requests)
     def _(request):
@@ -229,35 +246,22 @@
             latent_got.at[request],
             me,
         ).wait_recv()
-        block = draft * own_heads
-        head = lax.rem(lax.broadcasted_iota(jnp.int32, (near * block, value_width), 0), own_heads)
-        for half in range(2):
-            every = jnp.dot(
-                arrived[request, half * near : (half + 1) * near].reshape(near * block, latent_width),
-                matrix[half],
-                preferred_element_type=jnp.float32,
-            )
-            chosen = every[:, :value_width]
-            for h in range(1, own_heads):
-                chosen = jnp.where(head == h, every[:, h * value_width : (h + 1) * value_width], chosen)
-            mixed[request, half * near : (half + 1) * near] = chosen.astype(jnp.bfloat16).reshape(
-                near, block, value_width
-            )
-
-        @pl.loop(1, near)
-        def _(step):
-            other = lax.rem(seat + step, near)
-            for half in range(2):
-                copy_to(
-                    mixed.at[request, half * near + other],
-                    back_ref.at[request, half * near + seat],
-                    mixed_sent.at[request],
-                    mixed_got.at[request],
-                    side * near + other,
-                ).start()
-
-        for half in range(2):
-            back_ref[request, half * near + seat] = mixed[request, half * near + seat]
+        raise_values(request, side)
+
+        @pl.when(request == 0)
+        def _():
+            across.wait_recv()
+            for swap in swaps:
+                swap.start()
+
+    for swap in swaps:
+        swap.wait_recv()
+    for h in range(own_heads):
+        matrix[1 - side, :, h * value_width : (h + 1) * value_width] = far_matrix[h]
+
+    @pl.loop(0, requests)
+    def _(request):
+        raise_values(request, 1 - side)
 
     across.wait_send()
     for swap in swaps:

time: 73.6 us -> 75.5 us (1.026)
  Pallas kernels: 67.6 us -> 69.5 us
    pallas_call x1, Pallas kernels: 67.6 us -> 69.5 us  [per_device(): pl.pallas_call(functools.partial(exchange_kernel, groups_of), out_shape=j...]
where the time goes in v4:
time: 75.5 us; the launch traced here: 75.4 us
  Pallas kernels  69.5 us (92%)
  matrix products  3.84 us (5%)
  local copies, waits for them, and re-layouts  1.97 us (3%)
    pallas_call x1, Pallas kernels, per_device(): pl.pallas_call(functools.partial(exchange_kernel, groups_of), out_shape=j...  69.5 us
    dot_general x1, matrix products, per_device(): jnp.einsum('qp,psk->qsk', choose, page_pool, preferred_element_type=jnp.b...  3.84 us

profile of v4, /device:TPU:0, one launch (start us, length us, event | category | flops | bytes accessed | tf_op | source)
XLA Modules:
  0.0 75.4 jit_solution(9254158785491251329)
XLA Ops:
  0.0 0.0 copy-start.3
  0.0 0.0 copy-start.2
  0.0 0.0 copy-start
  0.0 1.0 %reshape.14.table_ref = s32[256,1]{1,0:T(8,128)S(1)} reshape(s32[4,64]{1,0:T(4,128)} %param.11) | data formatting | bytes 2048 | tf_op jit(solution)/shard_map/reshape | solution.py:333
  1.0 0.0 copy-start.1
  1.0 3.8 %fusion.1 = bf16[16,16,576]{2,0,1:T(8,128)(2,1)S(1)} fusion(bf16[256,16,576]{0,2,1:T(8,128)(2,1)} %param.9, s32[16]{0:T(128)} %bitcast.14), kind=kOutput, calls=%fused_computation.2 | convolution fusion | flops 75501568 | bytes 5013568 | tf_op jit(solution)/shard_map/qp,psk->qsk/dot_general | solution.py:298
  4.8 0.1 copy.11.outgoing_ref
  4.9 0.0 copy-done.3
  4.9 0.0 copy-done.2
  4.9 0.0 copy-done
  4.9 0.0 copy-done.1
  5.0 69.5 %exchange.1 = bf16[4,16,32,128]{3,2,1,0:T(8,128)(2,1)S(1)} custom-call(s32[4]{0:T(128)S(1)} %copy-done.3, s32[256,1]{1,0:T(8,128)S(1)} %reshape.14.table_ref, bf16[4,4,576,128]{3,2,1,0:T(8,128)(2,1)S(1)} %bitcast.12, bf16[4,4,576]{2,1,0:T(4,128)(2,1)S(1)} %copy-done.2, bf16[16,576,256]{2,1,0:T(8,128)(2,1)} %bitcast.13, ...), custom_call_target="tpu_custom_call" | custom-call | tf_op jit(solution)/shard_map/exchange/pallas_call | solution.py:302
  74.5 0.9 %reshape.11 = bf16[4,16,4,1024]{3,2,1,0:T(4,128)(2,1)} reshape(bf16[4,16,32,128]{3,2,1,0:T(8,128)(2,1)S(1)} %exchange.1) | data formatting | bytes 1048576 | tf_op jit(solution)/shard_map/reshape | solution.py:340
Async XLA Ops:
  0.0 4.9 %copy-start.3 = (s32[4]{0:T(128)S(1)}, s32[4]{0:T(128)}, u32[]{:S(2)}) copy-start(s32[4]{0:T(128)} %length_ref.1) | copy-start | bytes 52
  0.0 4.9 %copy-start.2 = (bf16[4,4,576]{2,1,0:T(4,128)(2,1)S(1)}, bf16[4,4,576]{2,1,0:T(4,128)(2,1)}, u32[]{:S(2)}) copy-start(bf16[4,4,576]{2,1,0:T(4,128)(2,1)} %draft_ref.1) | copy-start | bytes 55300
  0.0 4.9 %copy-start = (bf16[4,4,128,576]{2,3,1,0:T(8,128)(2,1)S(1)}, bf16[4,4,128,576]{2,3,1,0:T(8,128)(2,1)}, u32[]{:S(2)}) copy-start(bf16[4,4,128,576]{2,3,1,0:T(8,128)(2,1)} %param.7) | copy-start | bytes 7077892
  1.0 4.0 %copy-start.1 = (bf16[8,512,128]{2,1,0:T(8,128)(2,1)S(1)}, bf16[8,512,128]{2,1,0:T(8,128)(2,1)}, u32[]{:S(2)}) copy-start(bf16[8,512,128]{2,1,0:T(8,128)(2,1)} %matrix_ref.1) | copy-start | bytes 3145732
